TPU v7x, 256 devices: a whole 4x4x8 slice. The times are simulated.
256 devices in a mesh: district: 16 (over x, z_hi), tile: 16 (over z_lo, y, core).
Axes of the slice: x: 4, y: 4, z: 8 (z_hi: 4, z_lo: 2; z = z_hi * 2 + z_lo), core: 2. Of those that a mesh axis runs over, the one named last changes fastest.
Arguments:
- parent_state: float32 [3, 256, 2048], P(None, 'district', 'tile'), may hold values from -6 to 6
- parent_depth: float32 [256, 2048], P('district', 'tile'), may hold values from 0.25 to 1
- child_state: float32 [3, 1024, 2048], P(None, 'district', 'tile'), may hold values from -6 to 6
- child_depth: float32 [1024, 2048], P('district', 'tile'), may hold values from 0.1 to 1
- child_wet: int32 [4, 1024, 2048], P(None, 'district', 'tile'), may hold values 0 or 1
- interior_state: float32 [3, 16384, 128], P(None, ('district', 'tile')), may hold values from -6 to 6
- interior_wet: int32 [4, 16384, 128], P(None, ('district', 'tile')), may hold values 0 or 1
- parent_anchor: int32 [16, 16, 2], P('district'), may hold values from 0 to 2044, as said below
- open_row: int32 [16384], P(('district', 'tile')), may hold values from 0 to 63
- open_col: int32 [16384], P(('district', 'tile')), may hold values from 0 to 96
- open_owner: int32 [16384, 1], P(('district', 'tile')), may hold values from 0 to 15; in each aligned block of 64 rows (0 to 63, 64 to 127, ...) at most 8 rows name the same one
- open_valid: int32 [16384], P(('district', 'tile')), may hold values 0 or 1
- open_conduct: float32 [16384], P(('district', 'tile')), may hold values from 0.1 to 0.5
- door_rows: int32 [256, 128], P(('district', 'tile')), may hold values from 0 to 63
Outputs:
- parent_final: float32 [3, 256, 2048], P(None, 'district', 'tile')
- child_final: float32 [3, 1024, 2048], P(None, 'district', 'tile')
- interior_final: float32 [3, 16384, 128], P(None, ('district', 'tile'))
Inputs may be any that keep to these rules, and one draw needn't show every extreme that they name: `open_owner`: tile indices within the opening's own district group; among the rows of one device no owner is named by more than 8 rows, padded ones included. `parent_anchor`: entry 0 is the same for all tiles of a district and leaves room for 2 rows within the district's 16 parent rows; entry 1 rises by 4 from one tile to the next and every window lies within the parent grid's columns; district 0's windows start at column 0 and the last district's end at the grid's last column.
All inputs are finite; a program needn't handle non-finite values. No bound on the sum of `child_wet` or of `interior_wet` or of `open_valid` on one device may be relied on, other than what follows from the above.
Results may differ from a plain program's by a relative error of at most 0.0003.
Values sent between devices are 32-bit elements; how exact they have to be, the bound alone decides.
No kernel may reach another device: no remote copies, remote signals or barrier semaphores. Data moves between devices by JAX's collectives and lax.ppermute only.
A program may use at most 64 MiB of HBM per device.

v0:
```python
import jax
import jax.numpy as jnp
from jax import lax
from jax.sharding import PartitionSpec as P

CX = 64
CY = 128
IY = 128
R = 32
STEPS = 4
CAP = 8
SEG = 32
WX = 2
WY = 4
courant = 0.3
nudging = 0.25
area_ratio = 0.0625


def padded_2(cells, sides, width):
    for axis, dim in sides:
        count = lax.axis_size(axis)
        ends = count - 1
        head = lax.slice_in_dim(cells, 0, width, axis=dim)
        tail = lax.slice_in_dim(cells, cells.shape[dim] - width, cells.shape[dim], axis=dim)
        cells = jnp.concatenate(
            [
                lax.ppermute(tail, axis, [(i, (i + 1) % count) for i in range(ends)]),
                cells,
                lax.ppermute(head, axis, [((i + 1) % count, i) for i in range(ends)]),
            ],
            axis=dim,
        )
    return cells


def advance(padded, wet_cells):
    surface = padded[0]
    east_flow = padded[1]
    north_flow = padded[2]
    wet_depth = padded[3]
    new_east = east_flow[1:-1, 2:-2] - courant * (surface[2:, 2:-2] - surface[:-2, 2:-2])
    new_north = north_flow[2:-2, 1:-1] - courant * (surface[2:-2, 2:] - surface[2:-2, :-2])
    flux_east = wet_depth[1:-1, 2:-2] * new_east
    flux_north = wet_depth[2:-2, 1:-1] * new_north
    new_surface = surface[2:-2, 2:-2] - courant * (
        flux_east[2:] - flux_east[:-2] + flux_north[:, 2:] - flux_north[:, :-2]
    )
    return (new_surface, wet_cells * new_east[1:-1], wet_cells * new_north[:, 1:-1])


def room_step(state, wet_cells):
    padded = jnp.pad(jnp.concatenate([state, wet_cells[None]], 0), ((0, 0), (2, 2), (2, 2)))
    return jnp.stack(advance(padded, wet_cells))


def ranks(owners, tile_count):
    matches = (owners[:, None] == jnp.arange(tile_count, dtype=jnp.int32)[None, :]).astype(
        jnp.int32
    )
    return jnp.sum(jnp.cumsum(matches, 0) * matches, 1) - 1


def place_rows(values, owners, slot_of, tile_count):
    empty = jnp.zeros((tile_count, CAP) + values.shape[1:], values.dtype)
    return empty.at[owners, slot_of].set(values)


def opening_flow(street, weights, face_rows):
    inflow = weights[..., None] * (jnp.repeat(street, 4, axis=-1) - face_rows)
    grouped = inflow.reshape(inflow.shape[:-1] + (inflow.shape[-1] // 4, 4))
    return (inflow, jnp.sum(grouped, -1) * area_ratio)


def absorb(surface, room_rows, street, weights):
    face_rows = surface[room_rows].reshape(weights.shape + (IY,))
    inflow, flux_back = opening_flow(street, weights, face_rows)
    return (surface.at[room_rows].add(inflow.reshape(-1, IY)), flux_back)


def body(
    parent_state,
    parent_depth,
    child_state,
    child_depth,
    child_wet,
    interior_state,
    interior_wet,
    parent_anchor,
    open_row,
    open_col,
    open_owner,
    open_valid,
    open_conduct,
    door_rows,
):
    tile_count = lax.axis_size("tile")
    my_tile = lax.axis_index("tile")
    requests = parent_anchor[0]
    anchor = requests[my_tile]
    owners = open_owner[:, 0]
    slot_of = ranks(owners, tile_count)
    cell_ids = (open_row * CY + open_col)[:, None] + jnp.arange(SEG, dtype=jnp.int32)[None, :]
    weights = place_rows(open_conduct * open_valid.astype(jnp.float32), owners, slot_of, tile_count)
    room_rows = door_rows[0]
    parent_now = parent_state
    child_now = child_state
    rooms_now = interior_state
    for section_index in range(STEPS):
        parent_stack = jnp.concatenate([parent_now, parent_depth[None]], 0)
        padded = padded_2(parent_stack, (("district", 1), ("tile", 2)), 2)
        surface, east_flow, north_flow = advance(padded, 1.0)
        parent_now = jnp.stack([surface, east_flow, north_flow])
        district_rows = lax.all_gather(surface, "tile", axis=1, tiled=True)
        window = lax.dynamic_slice(district_rows, (anchor[0], anchor[1]), (WX, WY))
        target = jnp.broadcast_to(window[:, None, :, None], (WX, R, WY, R)).reshape(CX, CY)
        wet_now = child_wet[section_index].astype(jnp.float32)
        child_stack = jnp.concatenate([child_now, (child_depth * wet_now)[None]], 0)
        padded = padded_2(child_stack, (("district", 1), ("tile", 2)), 2)
        surface, east_flow, north_flow = advance(padded, wet_now)
        surface = surface + nudging * (target - surface)
        rooms_now = room_step(rooms_now, interior_wet[section_index].astype(jnp.float32))
        flat_level = surface.reshape(-1)
        street = place_rows(flat_level[cell_ids], owners, slot_of, tile_count)
        inbound, inweights = (
            lax.all_to_all(
                street.reshape(tile_count, CAP * SEG),
                "tile",
                split_axis=0,
                concat_axis=0,
                tiled=True,
            ),
            lax.all_to_all(weights, "tile", split_axis=0, concat_axis=0, tiled=True),
        )
        inbound = inbound.reshape(tile_count, CAP, SEG)
        room_surface, flux_back = absorb(rooms_now[0], room_rows, inbound, inweights)
        returned = lax.all_to_all(
            flux_back.reshape(tile_count, CAP * SEG),
            "tile",
            split_axis=0,
            concat_axis=0,
            tiled=True,
        )
        returned = returned.reshape(tile_count, CAP, SEG)
        rooms_now = rooms_now.at[0].set(room_surface)
        flat_level = flat_level.at[cell_ids].add(-returned[owners, slot_of])
        child_now = jnp.stack([flat_level.reshape(CX, CY), east_flow, north_flow])
    return (parent_now, child_now, rooms_now)


def solution(mesh):
    return jax.shard_map(
        body,
        mesh=mesh,
        in_specs=(
            P(None, "district", "tile"),
            P("district", "tile"),
            P(None, "district", "tile"),
            P("district", "tile"),
            P(None, "district", "tile"),
            P(None, ("district", "tile"), None),
            P(None, ("district", "tile"), None),
            P("district", None, None),
            P(("district", "tile")),
            P(("district", "tile")),
            P(("district", "tile"), None),
            P(("district", "tile")),
            P(("district", "tile")),
            P(("district", "tile"), None),
        ),
        out_specs=(
            P(None, "district", "tile"),
            P(None, "district", "tile"),
            P(None, ("district", "tile"), None),
        ),
        check_vma=False,
    )
```

profile of v0, /device:TPU:67, one launch (start us, length us, event | category | flops | bytes accessed | tf_op | source)
XLA Modules:
  0.0 467.1 jit_solution(14156101166894164927)
XLA Ops:
  1.4 6.1 %collective-permute-start = (f32[4,2,128]{2,1,0:T(2,128)S(1)}, f32[4,2,128]{2,1,0:T(2,128)S(1)}, u32[]{:S(2)}, u32[]{:S(2)}) collective-permute-start(f32[4,2,128]{2,1,0:T(2,128)S(1)} %get-tuple-element.203), channel_id=1, source_target_pairs={{0,16},{16,32},{32,48},{48,64},{64,80},{80,96},{96,112},{112,128},... | collective-permute-start | bytes 12296 | tf_op jit(solution)/shard_map/ppermute | solution.py:28
  10.4 5.5 %collective-permute-start.16 = (f32[4,2,128]{2,1,0:T(2,128)S(1)}, f32[4,2,128]{2,1,0:T(2,128)S(1)}, u32[]{:S(2)}, u32[]{:S(2)}) collective-permute-start(f32[4,2,128]{2,1,0:T(2,128)S(1)} %get-tuple-element.171), channel_id=1, source_target_pairs={{0,16},{16,32},{32,48},{48,64},{64,80},{80,96},{96,112},{112,128},... | collective-permute-start | bytes 12296 | tf_op jit(solution)/shard_map/ppermute | solution.py:28
  23.1 6.5 %all-to-all-start = ((f32[16,1,8]{2,1,0:T(1,128)}), f32[16,1,8]{2,1,0:T(1,128)S(1)}, u32[]{:S(2)}, u32[]{:S(2)}) async-start(f32[16,1,8]{2,1,0:T(1,128)} %copy.81), calls=%async_computation | async-start | bytes 16384 | tf_op jit(solution)/shard_map/all_to_all | solution.py:133
  39.6 3.5 collective-permute-start.2
  45.2 3.6 collective-permute-start.18
  51.3 20.3 %all_gather.12 = f32[16,2048]{1,0:T(8,128)S(1)} all-gather(f32[16,128]{1,0:T(8,128)S(1)} %fusion.135), channel_id=1, replica_groups=mesh['district'=16,'tile'=16] {'tile'}, dimensions={1}, use_global_device_ids=true | all-gather | bytes 139264 | tf_op jit(solution)/shard_map/all_gather | solution.py:114
  72.0 5.8 %collective-permute-start.4 = (f32[4,2,128]{2,1,0:T(2,128)S(1)}, f32[4,2,128]{2,1,0:T(2,128)S(1)}, u32[]{:S(2)}, u32[]{:S(2)}) collective-permute-start(f32[4,2,128]{2,1,0:T(2,128)S(1)} %get-tuple-element.201), channel_id=1, source_target_pairs={{0,16},{16,32},{32,48},{48,64},{64,80},{80,96},{96,112},{112,128},... | collective-permute-start | bytes 12296 | tf_op jit(solution)/shard_map/ppermute | solution.py:28
  80.0 4.1 collective-permute-done.5
  95.2 4.3 collective-permute-start.9
  99.5 11.8 %gather_fusion = f32[2048]{0:T(1024)S(1)} fusion(f32[8192]{0:T(1024)S(1)} %add_bitcast_fusion.3, s32[2048]{0:T(1024)S(1)} %broadcast_clamp_fusion), kind=kCustom, calls=%fused_computation | custom fusion | bytes 24576 | tf_op jit(solution)/shard_map/gather | solution.py:124
  111.4 3.6 scatter_fusion.1
  115.7 8.8 %all-to-all-start.1 = ((f32[16,1,256]{2,1,0:T(1,128)}), f32[16,1,256]{2,1,0:T(1,128)S(1)}, u32[]{:S(2)}, u32[]{:S(2)}) async-start(f32[16,1,256]{2,1,0:T(1,128)} %all_to_all.51), calls=%async_computation.1 | async-start | bytes 32768 | tf_op jit(solution)/shard_map/all_to_all | solution.py:126
  124.6 3.5 collective-permute-start.10
  140.3 19.2 %all_gather.13 = f32[16,2048]{1,0:T(8,128)S(1)} all-gather(f32[16,128]{1,0:T(8,128)S(1)} %fusion.133), channel_id=1, replica_groups=mesh['district'=16,'tile'=16] {'tile'}, dimensions={1}, use_global_device_ids=true | all-gather | bytes 139264 | tf_op jit(solution)/shard_map/all_gather | solution.py:114
  164.2 17.7 %all_gather.14 = f32[16,2048]{1,0:T(8,128)S(1)} all-gather(f32[16,128]{1,0:T(8,128)S(1)} %fusion.131), channel_id=1, replica_groups=mesh['district'=16,'tile'=16] {'tile'}, dimensions={1}, use_global_device_ids=true | all-gather | bytes 139264 | tf_op jit(solution)/shard_map/all_gather | solution.py:114
  183.3 18.6 %all_gather.15 = f32[16,2048]{1,0:T(8,128)S(1)} all-gather(f32[16,128]{1,0:T(8,128)S(1)} %fusion.129), channel_id=1, replica_groups=mesh['district'=16,'tile'=16] {'tile'}, dimensions={1}, use_global_device_ids=true | all-gather | bytes 139264 | tf_op jit(solution)/shard_map/all_gather | solution.py:114
  206.1 3.5 all-to-all-start.2
  209.7 5.7 %all-to-all-done.2 = f32[16,1,256]{2,1,0:T(1,128)S(1)} async-done(((f32[16,1,256]{2,1,0:T(1,128)}), f32[16,1,256]{2,1,0:T(1,128)S(1)}, u32[]{:S(2)}, u32[]{:S(2)}) %all-to-all-start.2) | async-done | bytes 16416 | tf_op jit(solution)/shard_map/all_to_all | solution.py:137
  216.4 14.7 %scatter_fusion.2 = f32[8192]{0:T(1024)S(1)} fusion(f32[8192]{0:T(1024)S(1)} %add_bitcast_fusion.3, s32[2048]{0:T(1024)S(1)} %reshape.550, f32[2048]{0:T(1024)S(1)} %reshape.552), kind=kCustom, calls=%fused_computation.14 | custom fusion | flops 2048 | bytes 32768 | tf_op jit(solution)/shard_map/scatter-add | solution.py:146
  231.1 4.4 collective-permute-start.20
  238.4 3.6 collective-permute-done.21
  242.1 3.9 collective-permute-start.22
  253.1 11.8 %gather_fusion.3 = f32[2048]{0:T(1024)S(1)} fusion(f32[8192]{0:T(1024)S(1)} %add_bitcast_fusion.2, s32[2048]{0:T(1024)S(1)} %broadcast_clamp_fusion), kind=kCustom, calls=%fused_computation.3 | custom fusion | bytes 24576 | tf_op jit(solution)/shard_map/gather | solution.py:124
  264.9 3.6 scatter_fusion.3
  269.2 6.2 %all-to-all-start.3 = ((f32[16,1,256]{2,1,0:T(1,128)}), f32[16,1,256]{2,1,0:T(1,128)S(1)}, u32[]{:S(2)}, u32[]{:S(2)}) async-start(f32[16,1,256]{2,1,0:T(1,128)} %all_to_all.54), calls=%async_computation.3 | async-start | bytes 32768 | tf_op jit(solution)/shard_map/all_to_all | solution.py:126
  275.5 5.7 %all-to-all-done.3 = f32[16,1,256]{2,1,0:T(1,128)S(1)} async-done(((f32[16,1,256]{2,1,0:T(1,128)}), f32[16,1,256]{2,1,0:T(1,128)S(1)}, u32[]{:S(2)}, u32[]{:S(2)}) %all-to-all-start.3) | async-done | bytes 16416 | tf_op jit(solution)/shard_map/all_to_all | solution.py:126
  285.1 3.7 all-to-all-start.4
  288.8 5.8 %all-to-all-done.4 = f32[16,1,256]{2,1,0:T(1,128)S(1)} async-done(((f32[16,1,256]{2,1,0:T(1,128)}), f32[16,1,256]{2,1,0:T(1,128)S(1)}, u32[]{:S(2)}, u32[]{:S(2)}) %all-to-all-start.4) | async-done | bytes 16416 | tf_op jit(solution)/shard_map/all_to_all | solution.py:137
  295.6 14.5 %scatter_fusion.4 = f32[8192]{0:T(1024)S(1)} fusion(f32[8192]{0:T(1024)S(1)} %add_bitcast_fusion.2, s32[2048]{0:T(1024)S(1)} %reshape.550, f32[2048]{0:T(1024)S(1)} %reshape.574), kind=kCustom, calls=%fused_computation.17 | custom fusion | flops 2048 | bytes 32768 | tf_op jit(solution)/shard_map/scatter-add | solution.py:146
  316.4 4.8 %collective-permute-done.25 = f32[4,2,128]{2,1,0:T(2,128)S(1)} collective-permute-done((f32[4,2,128]{2,1,0:T(2,128)S(1)}, f32[4,2,128]{2,1,0:T(2,128)S(1)}, u32[]{:S(2)}, u32[]{:S(2)}) %collective-permute-start.25) | collective-permute-done | bytes 4128 | tf_op jit(solution)/shard_map/ppermute | solution.py:30
  321.3 3.7 collective-permute-start.26
  332.0 11.8 %gather_fusion.6 = f32[2048]{0:T(1024)S(1)} fusion(f32[8192]{0:T(1024)S(1)} %add_bitcast_fusion.1, s32[2048]{0:T(1024)S(1)} %broadcast_clamp_fusion), kind=kCustom, calls=%fused_computation.6 | custom fusion | bytes 24576 | tf_op jit(solution)/shard_map/gather | solution.py:124
  343.9 3.6 scatter_fusion.5
  348.2 6.2 %all-to-all-start.5 = ((f32[16,1,256]{2,1,0:T(1,128)}), f32[16,1,256]{2,1,0:T(1,128)S(1)}, u32[]{:S(2)}, u32[]{:S(2)}) async-start(f32[16,1,256]{2,1,0:T(1,128)} %all_to_all.57), calls=%async_computation.5 | async-start | bytes 32768 | tf_op jit(solution)/shard_map/all_to_all | solution.py:126
  354.4 5.7 %all-to-all-done.5 = f32[16,1,256]{2,1,0:T(1,128)S(1)} async-done(((f32[16,1,256]{2,1,0:T(1,128)}), f32[16,1,256]{2,1,0:T(1,128)S(1)}, u32[]{:S(2)}, u32[]{:S(2)}) %all-to-all-start.5) | async-done | bytes 16416 | tf_op jit(solution)/shard_map/all_to_all | solution.py:126
  364.0 3.7 all-to-all-start.6
  367.7 5.8 %all-to-all-done.6 = f32[16,1,256]{2,1,0:T(1,128)S(1)} async-done(((f32[16,1,256]{2,1,0:T(1,128)}), f32[16,1,256]{2,1,0:T(1,128)S(1)}, u32[]{:S(2)}, u32[]{:S(2)}) %all-to-all-start.6) | async-done | bytes 16416 | tf_op jit(solution)/shard_map/all_to_all | solution.py:137
  374.5 14.5 %scatter_fusion.6 = f32[8192]{0:T(1024)S(1)} fusion(f32[8192]{0:T(1024)S(1)} %add_bitcast_fusion.1, s32[2048]{0:T(1024)S(1)} %reshape.550, f32[2048]{0:T(1024)S(1)} %reshape.596), kind=kCustom, calls=%fused_computation.20 | custom fusion | flops 2048 | bytes 32768 | tf_op jit(solution)/shard_map/scatter-add | solution.py:146
  389.0 4.6 collective-permute-start.28
  395.6 4.5 collective-permute-done.29
  400.2 3.9 collective-permute-start.30
  411.1 11.8 %gather_fusion.9 = f32[2048]{0:T(1024)S(1)} fusion(f32[8192]{0:T(1024)S(1)} %add_bitcast_fusion, s32[2048]{0:T(1024)S(1)} %broadcast_clamp_fusion), kind=kCustom, calls=%fused_computation.9 | custom fusion | bytes 24576 | tf_op jit(solution)/shard_map/gather | solution.py:124
  423.0 3.6 scatter_fusion.7
  427.3 6.2 %all-to-all-start.7 = ((f32[16,1,256]{2,1,0:T(1,128)}), f32[16,1,256]{2,1,0:T(1,128)S(1)}, u32[]{:S(2)}, u32[]{:S(2)}) async-start(f32[16,1,256]{2,1,0:T(1,128)} %all_to_all.60), calls=%async_computation.7 | async-start | bytes 32768 | tf_op jit(solution)/shard_map/all_to_all | solution.py:126
  433.6 5.7 %all-to-all-done.7 = f32[16,1,256]{2,1,0:T(1,128)S(1)} async-done(((f32[16,1,256]{2,1,0:T(1,128)}), f32[16,1,256]{2,1,0:T(1,128)S(1)}, u32[]{:S(2)}, u32[]{:S(2)}) %all-to-all-start.7) | async-done | bytes 16416 | tf_op jit(solution)/shard_map/all_to_all | solution.py:126
  441.3 3.7 all-to-all-start.8
  446.4 4.5 all-to-all-done.8
  451.8 14.5 %scatter_fusion.8 = f32[8192]{0:T(1024)S(1)} fusion(f32[8192]{0:T(1024)S(1)} %add_bitcast_fusion, s32[2048]{0:T(1024)S(1)} %reshape.550, f32[2048]{0:T(1024)S(1)} %reshape.618), kind=kCustom, calls=%fused_computation.23 | custom fusion | flops 2048 | bytes 32768 | tf_op jit(solution)/shard_map/scatter-add | solution.py:146
  (313 shorter events, 108.2 us)
Async XLA Ops:
  0.6 28.9 %copy-start = (s32[1,16,2]{1,2,0:T(2,128)S(1)}, s32[1,16,2]{1,2,0:T(2,128)}, u32[]{:S(2)}) copy-start(s32[1,16,2]{1,2,0:T(2,128)} %param.29) | copy-start | bytes 388
  0.6 8.9 %copy-start.8 = (f32[64,128]{1,0:T(8,128)S(1)}, f32[64,128]{1,0:T(8,128)}, u32[]{:S(2)}) copy-start(f32[64,128]{1,0:T(8,128)} %param.25) | copy-start | bytes 98308
  1.4 37.5 %collective-permute-start = (f32[4,2,128]{2,1,0:T(2,128)S(1)}, f32[4,2,128]{2,1,0:T(2,128)S(1)}, u32[]{:S(2)}, u32[]{:S(2)}) collective-permute-start(f32[4,2,128]{2,1,0:T(2,128)S(1)} %get-tuple-element.203), channel_id=1, source_target_pairs={{0,16},{16,32},{32,48},{48,64},{64,80},{80,96},{96,112},{112,128},... | collective-permute-start | bytes 12296 | tf_op jit(solution)/shard_map/ppermute | solution.py:28
  7.5 31.4 %collective-permute-start.1 = (f32[4,2,128]{2,1,0:T(2,128)S(1)}, f32[4,2,128]{2,1,0:T(2,128)S(1)}, u32[]{:S(2)}, u32[]{:S(2)}) collective-permute-start(f32[4,2,128]{2,1,0:T(2,128)S(1)} %get-tuple-element.204), channel_id=1, source_target_pairs={{16,0},{32,16},{48,32},{64,48},{80,64},{96,80},{112,96},{128,112},... | collective-permute-start | bytes 12296 | tf_op jit(solution)/shard_map/ppermute | solution.py:30
  10.4 34.6 %collective-permute-start.16 = (f32[4,2,128]{2,1,0:T(2,128)S(1)}, f32[4,2,128]{2,1,0:T(2,128)S(1)}, u32[]{:S(2)}, u32[]{:S(2)}) collective-permute-start(f32[4,2,128]{2,1,0:T(2,128)S(1)} %get-tuple-element.171), channel_id=1, source_target_pairs={{0,16},{16,32},{32,48},{48,64},{64,80},{80,96},{96,112},{112,128},... | collective-permute-start | bytes 12296 | tf_op jit(solution)/shard_map/ppermute | solution.py:28
  15.9 29.2 %collective-permute-start.17 = (f32[4,2,128]{2,1,0:T(2,128)S(1)}, f32[4,2,128]{2,1,0:T(2,128)S(1)}, u32[]{:S(2)}, u32[]{:S(2)}) collective-permute-start(f32[4,2,128]{2,1,0:T(2,128)S(1)} %get-tuple-element.172), channel_id=1, source_target_pairs={{16,0},{32,16},{48,32},{64,48},{80,64},{96,80},{112,96},{128,112},... | collective-permute-start | bytes 12296 | tf_op jit(solution)/shard_map/ppermute | solution.py:30
  18.9 11.2 %copy-start.12 = (s32[64]{0:T(128)S(1)}, s32[64]{0:T(128)}, u32[]{:S(2)}) copy-start(s32[64]{0:T(128)} %param.31) | copy-start | bytes 772
  18.9 11.2 %copy-start.13 = (s32[64]{0:T(128)S(1)}, s32[64]{0:T(128)}, u32[]{:S(2)}) copy-start(s32[64]{0:T(128)} %param.30) | copy-start | bytes 772
  22.4 7.9 %copy-start.3 = (s32[4,64,128]{2,1,0:T(8,128)S(1)}, s32[4,64,128]{2,1,0:T(8,128)}, u32[]{:S(2)}) copy-start(s32[4,64,128]{2,1,0:T(8,128)} %param.28) | copy-start | bytes 393220
  23.1 14.5 %all-to-all-start = ((f32[16,1,8]{2,1,0:T(1,128)}), f32[16,1,8]{2,1,0:T(1,128)S(1)}, u32[]{:S(2)}, u32[]{:S(2)}) async-start(f32[16,1,8]{2,1,0:T(1,128)} %copy.81), calls=%async_computation | async-start | bytes 16384 | tf_op jit(solution)/shard_map/all_to_all | solution.py:133
  39.6 11.2 %collective-permute-start.2 = (f32[4,20,2]{2,1,0:T(8,128)S(1)}, f32[4,20,2]{2,1,0:T(8,128)S(1)}, u32[]{:S(2)}, u32[]{:S(2)}) collective-permute-start(f32[4,20,2]{2,1,0:T(8,128)S(1)} %get-tuple-element.195), channel_id=1, source_target_pairs={{0,1},{1,2},{2,3},{3,4},{4,5},{5,6},{6,7},{7,8},{8,9},{9,10},{10,1... | collective-permute-start | bytes 1928 | tf_op jit(solution)/shard_map/ppermute | solution.py:28
  43.2 7.7 %collective-permute-start.3 = (f32[4,20,2]{2,1,0:T(8,128)S(1)}, f32[4,20,2]{2,1,0:T(8,128)S(1)}, u32[]{:S(2)}, u32[]{:S(2)}) collective-permute-start(f32[4,20,2]{2,1,0:T(8,128)S(1)} %get-tuple-element.196), channel_id=1, source_target_pairs={{1,0},{2,1},{3,2},{4,3},{5,4},{6,5},{7,6},{8,7},{9,8},{10,9},{11,1... | collective-permute-start | bytes 1928 | tf_op jit(solution)/shard_map/ppermute | solution.py:30
  45.2 34.4 %collective-permute-start.18 = (f32[4,68,2]{2,1,0:T(8,128)S(1)}, f32[4,68,2]{2,1,0:T(8,128)S(1)}, u32[]{:S(2)}, u32[]{:S(2)}) collective-permute-start(f32[4,68,2]{2,1,0:T(8,128)S(1)} %get-tuple-element.143), channel_id=1, source_target_pairs={{0,1},{1,2},{2,3},{3,4},{4,5},{5,6},{6,7},{7,8},{8,9},{9,10},{10,1... | collective-permute-start | bytes 6536 | tf_op jit(solution)/shard_map/ppermute | solution.py:28
  48.9 30.8 %collective-permute-start.19 = (f32[4,68,2]{2,1,0:T(8,128)S(1)}, f32[4,68,2]{2,1,0:T(8,128)S(1)}, u32[]{:S(2)}, u32[]{:S(2)}) collective-permute-start(f32[4,68,2]{2,1,0:T(8,128)S(1)} %get-tuple-element.144), channel_id=1, source_target_pairs={{1,0},{2,1},{3,2},{4,3},{5,4},{6,5},{7,6},{8,7},{9,8},{10,9},{11,1... | collective-permute-start | bytes 6536 | tf_op jit(solution)/shard_map/ppermute | solution.py:30
  72.0 8.1 %collective-permute-start.4 = (f32[4,2,128]{2,1,0:T(2,128)S(1)}, f32[4,2,128]{2,1,0:T(2,128)S(1)}, u32[]{:S(2)}, u32[]{:S(2)}) collective-permute-start(f32[4,2,128]{2,1,0:T(2,128)S(1)} %get-tuple-element.201), channel_id=1, source_target_pairs={{0,16},{16,32},{32,48},{48,64},{64,80},{80,96},{96,112},{112,128},... | collective-permute-start | bytes 12296 | tf_op jit(solution)/shard_map/ppermute | solution.py:28
  77.7 6.5 %collective-permute-start.5 = (f32[4,2,128]{2,1,0:T(2,128)S(1)}, f32[4,2,128]{2,1,0:T(2,128)S(1)}, u32[]{:S(2)}, u32[]{:S(2)}) collective-permute-start(f32[4,2,128]{2,1,0:T(2,128)S(1)} %get-tuple-element.202), channel_id=1, source_target_pairs={{16,0},{32,16},{48,32},{64,48},{80,64},{96,80},{112,96},{128,112},... | collective-permute-start | bytes 12296 | tf_op jit(solution)/shard_map/ppermute | solution.py:30
  84.3 5.1 %collective-permute-start.6 = (f32[4,20,2]{2,1,0:T(8,128)S(1)}, f32[4,20,2]{2,1,0:T(8,128)S(1)}, u32[]{:S(2)}, u32[]{:S(2)}) collective-permute-start(f32[4,20,2]{2,1,0:T(8,128)S(1)} %get-tuple-element.193), channel_id=1, source_target_pairs={{0,1},{1,2},{2,3},{3,4},{4,5},{5,6},{6,7},{7,8},{8,9},{9,10},{10,1... | collective-permute-start | bytes 1928 | tf_op jit(solution)/shard_map/ppermute | solution.py:28
  87.3 5.4 %collective-permute-start.7 = (f32[4,20,2]{2,1,0:T(8,128)S(1)}, f32[4,20,2]{2,1,0:T(8,128)S(1)}, u32[]{:S(2)}, u32[]{:S(2)}) collective-permute-start(f32[4,20,2]{2,1,0:T(8,128)S(1)} %get-tuple-element.194), channel_id=1, source_target_pairs={{1,0},{2,1},{3,2},{4,3},{5,4},{6,5},{7,6},{8,7},{9,8},{10,9},{11,1... | collective-permute-start | bytes 1928 | tf_op jit(solution)/shard_map/ppermute | solution.py:30
  93.2 31.3 %collective-permute-start.8 = (f32[4,2,128]{2,1,0:T(2,128)S(1)}, f32[4,2,128]{2,1,0:T(2,128)S(1)}, u32[]{:S(2)}, u32[]{:S(2)}) collective-permute-start(f32[4,2,128]{2,1,0:T(2,128)S(1)} %get-tuple-element.199), channel_id=1, source_target_pairs={{0,16},{16,32},{32,48},{48,64},{64,80},{80,96},{96,112},{112,128},... | collective-permute-start | bytes 12296 | tf_op jit(solution)/shard_map/ppermute | solution.py:28
  95.2 29.4 %collective-permute-start.9 = (f32[4,2,128]{2,1,0:T(2,128)S(1)}, f32[4,2,128]{2,1,0:T(2,128)S(1)}, u32[]{:S(2)}, u32[]{:S(2)}) collective-permute-start(f32[4,2,128]{2,1,0:T(2,128)S(1)} %get-tuple-element.200), channel_id=1, source_target_pairs={{16,0},{32,16},{48,32},{64,48},{80,64},{96,80},{112,96},{128,112},... | collective-permute-start | bytes 12296 | tf_op jit(solution)/shard_map/ppermute | solution.py:30
  115.7 86.6 %all-to-all-start.1 = ((f32[16,1,256]{2,1,0:T(1,128)}), f32[16,1,256]{2,1,0:T(1,128)S(1)}, u32[]{:S(2)}, u32[]{:S(2)}) async-start(f32[16,1,256]{2,1,0:T(1,128)} %all_to_all.51), calls=%async_computation.1 | async-start | bytes 32768 | tf_op jit(solution)/shard_map/all_to_all | solution.py:126
  124.5 5.6 %copy-start.4 = (s32[4,64,128]{2,1,0:T(8,128)S(1)}, s32[4,64,128]{2,1,0:T(8,128)}, u32[]{:S(2)}) copy-start(s32[4,64,128]{2,1,0:T(8,128)} %param.26) | copy-start | bytes 393220
  124.6 5.6 %collective-permute-start.10 = (f32[4,20,2]{2,1,0:T(8,128)S(1)}, f32[4,20,2]{2,1,0:T(8,128)S(1)}, u32[]{:S(2)}, u32[]{:S(2)}) collective-permute-start(f32[4,20,2]{2,1,0:T(8,128)S(1)} %get-tuple-element.191), channel_id=1, source_target_pairs={{0,1},{1,2},{2,3},{3,4},{4,5},{5,6},{6,7},{7,8},{8,9},{9,10},{10,1... | collective-permute-start | bytes 1928 | tf_op jit(solution)/shard_map/ppermute | solution.py:28
  128.2 5.4 %collective-permute-start.11 = (f32[4,20,2]{2,1,0:T(8,128)S(1)}, f32[4,20,2]{2,1,0:T(8,128)S(1)}, u32[]{:S(2)}, u32[]{:S(2)}) collective-permute-start(f32[4,20,2]{2,1,0:T(8,128)S(1)} %get-tuple-element.192), channel_id=1, source_target_pairs={{1,0},{2,1},{3,2},{4,3},{5,4},{6,5},{7,6},{8,7},{9,8},{10,9},{11,1... | collective-permute-start | bytes 1928 | tf_op jit(solution)/shard_map/ppermute | solution.py:30
  134.1 25.6 %collective-permute-start.12 = (f32[4,2,128]{2,1,0:T(2,128)S(1)}, f32[4,2,128]{2,1,0:T(2,128)S(1)}, u32[]{:S(2)}, u32[]{:S(2)}) collective-permute-start(f32[4,2,128]{2,1,0:T(2,128)S(1)} %get-tuple-element.197), channel_id=1, source_target_pairs={{0,16},{16,32},{32,48},{48,64},{64,80},{80,96},{96,112},{112,128},... | collective-permute-start | bytes 12296 | tf_op jit(solution)/shard_map/ppermute | solution.py:28
  137.3 22.5 %collective-permute-start.13 = (f32[4,2,128]{2,1,0:T(2,128)S(1)}, f32[4,2,128]{2,1,0:T(2,128)S(1)}, u32[]{:S(2)}, u32[]{:S(2)}) collective-permute-start(f32[4,2,128]{2,1,0:T(2,128)S(1)} %get-tuple-element.198), channel_id=1, source_target_pairs={{16,0},{32,16},{48,32},{64,48},{80,64},{96,80},{112,96},{128,112},... | collective-permute-start | bytes 12296 | tf_op jit(solution)/shard_map/ppermute | solution.py:30
  159.8 22.4 %collective-permute-start.14 = (f32[4,20,2]{2,1,0:T(8,128)S(1)}, f32[4,20,2]{2,1,0:T(8,128)S(1)}, u32[]{:S(2)}, u32[]{:S(2)}) collective-permute-start(f32[4,20,2]{2,1,0:T(8,128)S(1)} %get-tuple-element.189), channel_id=1, source_target_pairs={{0,1},{1,2},{2,3},{3,4},{4,5},{5,6},{6,7},{7,8},{8,9},{9,10},{10,1... | collective-permute-start | bytes 1928 | tf_op jit(solution)/shard_map/ppermute | solution.py:28
  161.8 20.5 %collective-permute-start.15 = (f32[4,20,2]{2,1,0:T(8,128)S(1)}, f32[4,20,2]{2,1,0:T(8,128)S(1)}, u32[]{:S(2)}, u32[]{:S(2)}) collective-permute-start(f32[4,20,2]{2,1,0:T(8,128)S(1)} %get-tuple-element.190), channel_id=1, source_target_pairs={{1,0},{2,1},{3,2},{4,3},{5,4},{6,5},{7,6},{8,7},{9,8},{10,9},{11,1... | collective-permute-start | bytes 1928 | tf_op jit(solution)/shard_map/ppermute | solution.py:30
  206.1 9.3 %all-to-all-start.2 = ((f32[16,1,256]{2,1,0:T(1,128)}), f32[16,1,256]{2,1,0:T(1,128)S(1)}, u32[]{:S(2)}, u32[]{:S(2)}) async-start(f32[16,1,256]{2,1,0:T(1,128)} %mul.476), calls=%async_computation.2 | async-start | bytes 32768 | tf_op jit(solution)/shard_map/all_to_all | solution.py:137
  231.1 7.3 %collective-permute-start.20 = (f32[4,2,128]{2,1,0:T(2,128)S(1)}, f32[4,2,128]{2,1,0:T(2,128)S(1)}, u32[]{:S(2)}, u32[]{:S(2)}) collective-permute-start(f32[4,2,128]{2,1,0:T(2,128)S(1)} %get-tuple-element.167), channel_id=1, source_target_pairs={{0,16},{16,32},{32,48},{48,64},{64,80},{80,96},{96,112},{112,128},... | collective-permute-start | bytes 12296 | tf_op jit(solution)/shard_map/ppermute | solution.py:28
  235.5 6.5 %collective-permute-start.21 = (f32[4,2,128]{2,1,0:T(2,128)S(1)}, f32[4,2,128]{2,1,0:T(2,128)S(1)}, u32[]{:S(2)}, u32[]{:S(2)}) collective-permute-start(f32[4,2,128]{2,1,0:T(2,128)S(1)} %get-tuple-element.168), channel_id=1, source_target_pairs={{16,0},{32,16},{48,32},{64,48},{80,64},{96,80},{112,96},{128,112},... | collective-permute-start | bytes 12296 | tf_op jit(solution)/shard_map/ppermute | solution.py:30
  242.1 7.2 %collective-permute-start.22 = (f32[4,68,2]{2,1,0:T(8,128)S(1)}, f32[4,68,2]{2,1,0:T(8,128)S(1)}, u32[]{:S(2)}, u32[]{:S(2)}) collective-permute-start(f32[4,68,2]{2,1,0:T(8,128)S(1)} %get-tuple-element.141), channel_id=1, source_target_pairs={{0,1},{1,2},{2,3},{3,4},{4,5},{5,6},{6,7},{7,8},{8,9},{9,10},{10,1... | collective-permute-start | bytes 6536 | tf_op jit(solution)/shard_map/ppermute | solution.py:28
  246.0 6.5 %collective-permute-start.23 = (f32[4,68,2]{2,1,0:T(8,128)S(1)}, f32[4,68,2]{2,1,0:T(8,128)S(1)}, u32[]{:S(2)}, u32[]{:S(2)}) collective-permute-start(f32[4,68,2]{2,1,0:T(8,128)S(1)} %get-tuple-element.142), channel_id=1, source_target_pairs={{1,0},{2,1},{3,2},{4,3},{5,4},{6,5},{7,6},{8,7},{9,8},{10,9},{11,1... | collective-permute-start | bytes 6536 | tf_op jit(solution)/shard_map/ppermute | solution.py:30
  269.2 12.0 %all-to-all-start.3 = ((f32[16,1,256]{2,1,0:T(1,128)}), f32[16,1,256]{2,1,0:T(1,128)S(1)}, u32[]{:S(2)}, u32[]{:S(2)}) async-start(f32[16,1,256]{2,1,0:T(1,128)} %all_to_all.54), calls=%async_computation.3 | async-start | bytes 32768 | tf_op jit(solution)/shard_map/all_to_all | solution.py:126
  285.1 9.5 %all-to-all-start.4 = ((f32[16,1,256]{2,1,0:T(1,128)}), f32[16,1,256]{2,1,0:T(1,128)S(1)}, u32[]{:S(2)}, u32[]{:S(2)}) async-start(f32[16,1,256]{2,1,0:T(1,128)} %mul.477), calls=%async_computation.4 | async-start | bytes 32768 | tf_op jit(solution)/shard_map/all_to_all | solution.py:137
  310.1 6.3 %collective-permute-start.24 = (f32[4,2,128]{2,1,0:T(2,128)S(1)}, f32[4,2,128]{2,1,0:T(2,128)S(1)}, u32[]{:S(2)}, u32[]{:S(2)}) collective-permute-start(f32[4,2,128]{2,1,0:T(2,128)S(1)} %get-tuple-element.161), channel_id=1, source_target_pairs={{0,16},{16,32},{32,48},{48,64},{64,80},{80,96},{96,112},{112,128},... | collective-permute-start | bytes 12296 | tf_op jit(solution)/shard_map/ppermute | solution.py:28
  313.6 7.6 %collective-permute-start.25 = (f32[4,2,128]{2,1,0:T(2,128)S(1)}, f32[4,2,128]{2,1,0:T(2,128)S(1)}, u32[]{:S(2)}, u32[]{:S(2)}) collective-permute-start(f32[4,2,128]{2,1,0:T(2,128)S(1)} %get-tuple-element.162), channel_id=1, source_target_pairs={{16,0},{32,16},{48,32},{64,48},{80,64},{96,80},{112,96},{128,112},... | collective-permute-start | bytes 12296 | tf_op jit(solution)/shard_map/ppermute | solution.py:30
  321.3 6.9 %collective-permute-start.26 = (f32[4,68,2]{2,1,0:T(8,128)S(1)}, f32[4,68,2]{2,1,0:T(8,128)S(1)}, u32[]{:S(2)}, u32[]{:S(2)}) collective-permute-start(f32[4,68,2]{2,1,0:T(8,128)S(1)} %get-tuple-element.139), channel_id=1, source_target_pairs={{0,1},{1,2},{2,3},{3,4},{4,5},{5,6},{6,7},{7,8},{8,9},{9,10},{10,1... | collective-permute-start | bytes 6536 | tf_op jit(solution)/shard_map/ppermute | solution.py:28
  325.0 6.5 %collective-permute-start.27 = (f32[4,68,2]{2,1,0:T(8,128)S(1)}, f32[4,68,2]{2,1,0:T(8,128)S(1)}, u32[]{:S(2)}, u32[]{:S(2)}) collective-permute-start(f32[4,68,2]{2,1,0:T(8,128)S(1)} %get-tuple-element.140), channel_id=1, source_target_pairs={{1,0},{2,1},{3,2},{4,3},{5,4},{6,5},{7,6},{8,7},{9,8},{10,9},{11,1... | collective-permute-start | bytes 6536 | tf_op jit(solution)/shard_map/ppermute | solution.py:30
  348.2 11.9 %all-to-all-start.5 = ((f32[16,1,256]{2,1,0:T(1,128)}), f32[16,1,256]{2,1,0:T(1,128)S(1)}, u32[]{:S(2)}, u32[]{:S(2)}) async-start(f32[16,1,256]{2,1,0:T(1,128)} %all_to_all.57), calls=%async_computation.5 | async-start | bytes 32768 | tf_op jit(solution)/shard_map/all_to_all | solution.py:126
  364.0 9.5 %all-to-all-start.6 = ((f32[16,1,256]{2,1,0:T(1,128)}), f32[16,1,256]{2,1,0:T(1,128)S(1)}, u32[]{:S(2)}, u32[]{:S(2)}) async-start(f32[16,1,256]{2,1,0:T(1,128)} %mul.478), calls=%async_computation.6 | async-start | bytes 32768 | tf_op jit(solution)/shard_map/all_to_all | solution.py:137
  389.0 6.6 %collective-permute-start.28 = (f32[4,2,128]{2,1,0:T(2,128)S(1)}, f32[4,2,128]{2,1,0:T(2,128)S(1)}, u32[]{:S(2)}, u32[]{:S(2)}) collective-permute-start(f32[4,2,128]{2,1,0:T(2,128)S(1)} %get-tuple-element.155), channel_id=1, source_target_pairs={{0,16},{16,32},{32,48},{48,64},{64,80},{80,96},{96,112},{112,128},... | collective-permute-start | bytes 12296 | tf_op jit(solution)/shard_map/ppermute | solution.py:28
  393.6 6.5 %collective-permute-start.29 = (f32[4,2,128]{2,1,0:T(2,128)S(1)}, f32[4,2,128]{2,1,0:T(2,128)S(1)}, u32[]{:S(2)}, u32[]{:S(2)}) collective-permute-start(f32[4,2,128]{2,1,0:T(2,128)S(1)} %get-tuple-element.156), channel_id=1, source_target_pairs={{16,0},{32,16},{48,32},{64,48},{80,64},{96,80},{112,96},{128,112},... | collective-permute-start | bytes 12296 | tf_op jit(solution)/shard_map/ppermute | solution.py:30
  400.2 7.2 %collective-permute-start.30 = (f32[4,68,2]{2,1,0:T(8,128)S(1)}, f32[4,68,2]{2,1,0:T(8,128)S(1)}, u32[]{:S(2)}, u32[]{:S(2)}) collective-permute-start(f32[4,68,2]{2,1,0:T(8,128)S(1)} %get-tuple-element.137), channel_id=1, source_target_pairs={{0,1},{1,2},{2,3},{3,4},{4,5},{5,6},{6,7},{7,8},{8,9},{9,10},{10,1... | collective-permute-start | bytes 6536 | tf_op jit(solution)/shard_map/ppermute | solution.py:28
  404.1 6.5 %collective-permute-start.31 = (f32[4,68,2]{2,1,0:T(8,128)S(1)}, f32[4,68,2]{2,1,0:T(8,128)S(1)}, u32[]{:S(2)}, u32[]{:S(2)}) collective-permute-start(f32[4,68,2]{2,1,0:T(8,128)S(1)} %get-tuple-element.138), channel_id=1, source_target_pairs={{1,0},{2,1},{3,2},{4,3},{5,4},{6,5},{7,6},{8,7},{9,8},{10,9},{11,1... | collective-permute-start | bytes 6536 | tf_op jit(solution)/shard_map/ppermute | solution.py:30
  427.3 12.0 %all-to-all-start.7 = ((f32[16,1,256]{2,1,0:T(1,128)}), f32[16,1,256]{2,1,0:T(1,128)S(1)}, u32[]{:S(2)}, u32[]{:S(2)}) async-start(f32[16,1,256]{2,1,0:T(1,128)} %all_to_all.60), calls=%async_computation.7 | async-start | bytes 32768 | tf_op jit(solution)/shard_map/all_to_all | solution.py:126
  441.3 9.5 %all-to-all-start.8 = ((f32[16,1,256]{2,1,0:T(1,128)}), f32[16,1,256]{2,1,0:T(1,128)S(1)}, u32[]{:S(2)}, u32[]{:S(2)}) async-start(f32[16,1,256]{2,1,0:T(1,128)} %mul.479), calls=%async_computation.8 | async-start | bytes 32768 | tf_op jit(solution)/shard_map/all_to_all | solution.py:137
  446.4 5.4 %copy-start.6 = (f32[3,64,128]{2,1,0:T(8,128)}, f32[3,64,128]{2,1,0:T(8,128)S(1)}, u32[]{:S(2)}) copy-start(f32[3,64,128]{2,1,0:T(8,128)S(1)} %bitcast_dynamic-update-slice_fusion) | copy-start | bytes 294916
  (8 other events, 11.7 us)
where the time goes:
time: 469 us; the launch traced here: 467 us
  starting transfers between devices  147 us (31%)
  local copies, waits for them, and re-layouts  91 us (19%)
  blocking collectives  75.9 us (16%)
  other arithmetic  75 us (16%)
  waiting for transfers between devices  72.2 us (15%)
  between operations  6.22 us (1%)
    all_gather x4, blocking collectives, body(): district_rows = lax.all_gather(surface, 'tile', axis=1, tiled=True)  75.9 us
    ppermute x16, starting transfers between devices, padded_2(): lax.ppermute(tail, axis, [(i, (i + 1) % count) for i in range(ends)])  61.9 us
    scatter-add x4, other arithmetic, body(): flat_level = flat_level.at[cell_ids].add(-returned[owners, slot_of])  58.4 us
    gather x8, local copies, waits for them, and re-layouts, body(): street = place_rows(flat_level[cell_ids], owners, slot_of, tile_count)  47.4 us
    ppermute x16, starting transfers between devices, padded_2(): lax.ppermute(head, axis, [((i + 1) % count, i) for i in range(ends)])  36.4 us
    ppermute x16, waiting for transfers between devices, padded_2(): lax.ppermute(head, axis, [((i + 1) % count, i) for i in range(ends)])  33.3 us
    all_to_all x4, starting transfers between devices, body(): lax.all_to_all(street.reshape(tile_count, CAP * SEG), 'tile', split_axis=...  27.4 us
    all_to_all x4, waiting for transfers between devices, body(): lax.all_to_all(flux_back.reshape(tile_count, CAP * SEG), 'tile', split_ax...  21.7 us
  transfers between devices with their start and end apart: 41, of which 16 were waited for; matrix products, arithmetic and copies ran while one was open for 7% of the time, Pallas kernels for 0%

commit v1 on v0

--- a/solution.py
+++ b/solution.py
@@ -111,7 +111,9 @@
         padded = padded_2(parent_stack, (("district", 1), ("tile", 2)), 2)
         surface, east_flow, north_flow = advance(padded, 1.0)
         parent_now = jnp.stack([surface, east_flow, north_flow])
-        district_rows = lax.all_gather(surface, "tile", axis=1, tiled=True)
+        district_rows = jnp.concatenate(
+            lax.all_to_all(jnp.stack([surface] * lax.axis_size("tile")), "tile", 0, 0), axis=1
+        )
         window = lax.dynamic_slice(district_rows, (anchor[0], anchor[1]), (WX, WY))
         target = jnp.broadcast_to(window[:, None, :, None], (WX, R, WY, R)).reshape(CX, CY)
         wet_now = child_wet[section_index].astype(jnp.float32)

time: 469 us -> 446 us (0.951)
  blocking collectives: 75.9 us -> 0 us
  waiting for transfers between devices: 72.2 us -> 97.4 us
  starting transfers between devices: 147 us -> 170 us
    all_gather x4 -> x0, blocking collectives: 75.9 us -> none  [body(): district_rows = lax.all_gather(surface, 'tile', axis=1, tiled=True)]
    all_to_all x0 -> x4, starting transfers between devices: none -> 27.6 us  [body(): lax.all_to_all(jnp.stack([surface] * lax.axis_size('tile')), 'tile', 0, 0)]
    all_to_all x0 -> x4, waiting for transfers between devices: none -> 11.8 us  [body(): lax.all_to_all(jnp.stack([surface] * lax.axis_size('tile')), 'tile', 0, 0)]
    ppermute x16, waiting for transfers between devices: 33.3 us -> 41.2 us  [padded_2(): lax.ppermute(head, axis, [((i + 1) % count, i) for i in range(ends)])]
    all_to_all x4, waiting for transfers between devices: 17.1 us -> 22.7 us  [body(): lax.all_to_all(street.reshape(tile_count, CAP * SEG), 'tile', split_axis=...]
    all_to_all x4, starting transfers between devices: 27.4 us -> 22.6 us  [body(): lax.all_to_all(street.reshape(tile_count, CAP * SEG), 'tile', split_axis=...]
  transfers between devices with their start and end apart: 41 -> 45, of which waited for: 16 -> 22; matrix products, arithmetic and copies ran while one was open for 7% -> 8% of each run, Pallas kernels for 0% -> 0%
where the time goes in v1:
time: 446 us; the launch traced here: 443 us
  starting transfers between devices  170 us (38%)
  waiting for transfers between devices  97.4 us (22%)
  local copies, waits for them, and re-layouts  93.7 us (21%)
  other arithmetic  75.2 us (17%)
  between operations  6.19 us (1%)
    ppermute x16, starting transfers between devices, padded_2(): lax.ppermute(tail, axis, [(i, (i + 1) % count) for i in range(ends)])  62.6 us
    scatter-add x4, other arithmetic, body(): flat_level = flat_level.at[cell_ids].add(-returned[owners, slot_of])  58.4 us
    gather x8, local copies, waits for them, and re-layouts, body(): street = place_rows(flat_level[cell_ids], owners, slot_of, tile_count)  47.4 us
    ppermute x16, waiting for transfers between devices, padded_2(): lax.ppermute(head, axis, [((i + 1) % count, i) for i in range(ends)])  41.2 us
    ppermute x16, starting transfers between devices, padded_2(): lax.ppermute(head, axis, [((i + 1) % count, i) for i in range(ends)])  36.1 us
    all_to_all x4, starting transfers between devices, body(): lax.all_to_all(jnp.stack([surface] * lax.axis_size('tile')), 'tile', 0, 0)  27.6 us
    all_to_all x4, waiting for transfers between devices, body(): lax.all_to_all(street.reshape(tile_count, CAP * SEG), 'tile', split_axis=...  22.7 us
    all_to_all x4, starting transfers between devices, body(): lax.all_to_all(street.reshape(tile_count, CAP * SEG), 'tile', split_axis=...  22.6 us
  transfers between devices with their start and end apart: 45, of which 22 were waited for; matrix products, arithmetic and copies ran while one was open for 8% of the time, Pallas kernels for 0%

profile of v1, /device:TPU:67, one launch (start us, length us, event | category | flops | bytes accessed | tf_op | source)
XLA Modules:
  0.0 442.6 jit_solution(2965842821156440974)
XLA Ops:
  1.4 6.1 %collective-permute-start = (f32[4,2,128]{2,1,0:T(2,128)S(1)}, f32[4,2,128]{2,1,0:T(2,128)S(1)}, u32[]{:S(2)}, u32[]{:S(2)}) collective-permute-start(f32[4,2,128]{2,1,0:T(2,128)S(1)} %get-tuple-element.203), channel_id=1, source_target_pairs={{0,16},{16,32},{32,48},{48,64},{64,80},{80,96},{96,112},{112,128},... | collective-permute-start | bytes 12296 | tf_op jit(solution)/shard_map/ppermute | solution.py:28
  10.4 5.5 %collective-permute-start.16 = (f32[4,2,128]{2,1,0:T(2,128)S(1)}, f32[4,2,128]{2,1,0:T(2,128)S(1)}, u32[]{:S(2)}, u32[]{:S(2)}) collective-permute-start(f32[4,2,128]{2,1,0:T(2,128)S(1)} %get-tuple-element.171), channel_id=1, source_target_pairs={{0,16},{16,32},{32,48},{48,64},{64,80},{80,96},{96,112},{112,128},... | collective-permute-start | bytes 12296 | tf_op jit(solution)/shard_map/ppermute | solution.py:28
  23.1 6.5 %all-to-all-start.1 = ((f32[16,1,8]{2,1,0:T(1,128)}), f32[16,1,8]{2,1,0:T(1,128)S(1)}, u32[]{:S(2)}, u32[]{:S(2)}) async-start(f32[16,1,8]{2,1,0:T(1,128)} %copy.86), calls=%async_computation.1 | async-start | bytes 16384 | tf_op jit(solution)/shard_map/all_to_all | solution.py:135
  49.1 5.7 %collective-permute-start.4 = (f32[4,2,128]{2,1,0:T(2,128)S(1)}, f32[4,2,128]{2,1,0:T(2,128)S(1)}, u32[]{:S(2)}, u32[]{:S(2)}) collective-permute-start(f32[4,2,128]{2,1,0:T(2,128)S(1)} %get-tuple-element.201), channel_id=1, source_target_pairs={{0,16},{16,32},{32,48},{48,64},{64,80},{80,96},{96,112},{112,128},... | collective-permute-start | bytes 12296 | tf_op jit(solution)/shard_map/ppermute | solution.py:28
  61.9 7.4 %all-to-all-start = ((f32[16,16,128]{2,1,0:T(8,128)}), f32[16,16,128]{2,1,0:T(8,128)S(1)}, u32[]{:S(2)}, u32[]{:S(2)}) async-start(f32[16,16,128]{2,1,0:T(8,128)} %stack.97), calls=%async_computation | async-start | bytes 262144 | tf_op jit(solution)/shard_map/all_to_all | solution.py:115
  69.4 3.5 collective-permute-start.6
  78.8 5.8 %collective-permute-start.8 = (f32[4,2,128]{2,1,0:T(2,128)S(1)}, f32[4,2,128]{2,1,0:T(2,128)S(1)}, u32[]{:S(2)}, u32[]{:S(2)}) collective-permute-start(f32[4,2,128]{2,1,0:T(2,128)S(1)} %get-tuple-element.199), channel_id=1, source_target_pairs={{0,16},{16,32},{32,48},{48,64},{64,80},{80,96},{96,112},{112,128},... | collective-permute-start | bytes 12296 | tf_op jit(solution)/shard_map/ppermute | solution.py:28
  86.5 4.5 %collective-permute-done.9 = f32[4,2,128]{2,1,0:T(2,128)S(1)} collective-permute-done((f32[4,2,128]{2,1,0:T(2,128)S(1)}, f32[4,2,128]{2,1,0:T(2,128)S(1)}, u32[]{:S(2)}, u32[]{:S(2)}) %collective-permute-start.9) | collective-permute-done | bytes 4128 | tf_op jit(solution)/shard_map/ppermute | solution.py:30
  102.3 4.3 collective-permute-start.13
  120.0 10.5 %all-to-all-start.4 = ((f32[16,16,128]{2,1,0:T(8,128)}), f32[16,16,128]{2,1,0:T(8,128)S(1)}, u32[]{:S(2)}, u32[]{:S(2)}) async-start(f32[16,16,128]{2,1,0:T(8,128)} %stack.100), calls=%async_computation.4 | async-start | bytes 262144 | tf_op jit(solution)/shard_map/all_to_all | solution.py:115
  130.9 11.8 %gather_fusion = f32[2048]{0:T(1024)S(1)} fusion(f32[8192]{0:T(1024)S(1)} %add_bitcast_fusion.3, s32[2048]{0:T(1024)S(1)} %broadcast_clamp_fusion), kind=kCustom, calls=%fused_computation | custom fusion | bytes 24576 | tf_op jit(solution)/shard_map/gather | solution.py:126
  142.8 3.6 scatter_fusion.1
  147.7 5.7 %all-to-all-start.7 = ((f32[16,16,128]{2,1,0:T(8,128)}), f32[16,16,128]{2,1,0:T(8,128)S(1)}, u32[]{:S(2)}, u32[]{:S(2)}) async-start(f32[16,16,128]{2,1,0:T(8,128)} %stack.213), calls=%async_computation.7 | async-start | bytes 262144 | tf_op jit(solution)/shard_map/all_to_all | solution.py:115
  153.8 5.8 %all-to-all-done.7 = f32[16,16,128]{2,1,0:T(8,128)S(1)} async-done(((f32[16,16,128]{2,1,0:T(8,128)}), f32[16,16,128]{2,1,0:T(8,128)S(1)}, u32[]{:S(2)}, u32[]{:S(2)}) %all-to-all-start.7) | async-done | bytes 131104 | tf_op jit(solution)/shard_map/all_to_all | solution.py:115
  160.3 4.0 all-to-all-start.10
  164.5 5.9 %all-to-all-done.10 = f32[16,16,128]{2,1,0:T(8,128)S(1)} async-done(((f32[16,16,128]{2,1,0:T(8,128)}), f32[16,16,128]{2,1,0:T(8,128)S(1)}, u32[]{:S(2)}, u32[]{:S(2)}) %all-to-all-start.10) | async-done | bytes 131104 | tf_op jit(solution)/shard_map/all_to_all | solution.py:115
  170.5 4.0 all-to-all-start.2
  174.7 5.5 %all-to-all-done.2 = f32[16,1,256]{2,1,0:T(1,128)S(1)} async-done(((f32[16,1,256]{2,1,0:T(1,128)}), f32[16,1,256]{2,1,0:T(1,128)S(1)}, u32[]{:S(2)}, u32[]{:S(2)}) %all-to-all-start.2) | async-done | bytes 16416 | tf_op jit(solution)/shard_map/all_to_all | solution.py:128
  184.1 3.7 all-to-all-start.3
  187.9 5.8 %all-to-all-done.3 = f32[16,1,256]{2,1,0:T(1,128)S(1)} async-done(((f32[16,1,256]{2,1,0:T(1,128)}), f32[16,1,256]{2,1,0:T(1,128)S(1)}, u32[]{:S(2)}, u32[]{:S(2)}) %all-to-all-start.3) | async-done | bytes 16416 | tf_op jit(solution)/shard_map/all_to_all | solution.py:139
  194.6 14.7 %scatter_fusion.2 = f32[8192]{0:T(1024)S(1)} fusion(f32[8192]{0:T(1024)S(1)} %add_bitcast_fusion.3, s32[2048]{0:T(1024)S(1)} %reshape.590, f32[2048]{0:T(1024)S(1)} %reshape.592), kind=kCustom, calls=%fused_computation.14 | custom fusion | flops 2048 | bytes 32768 | tf_op jit(solution)/shard_map/scatter-add | solution.py:148
  209.4 4.5 %collective-permute-start.20 = (f32[4,2,128]{2,1,0:T(2,128)S(1)}, f32[4,2,128]{2,1,0:T(2,128)S(1)}, u32[]{:S(2)}, u32[]{:S(2)}) collective-permute-start(f32[4,2,128]{2,1,0:T(2,128)S(1)} %get-tuple-element.167), channel_id=1, source_target_pairs={{0,16},{16,32},{32,48},{48,64},{64,80},{80,96},{96,112},{112,128},... | collective-permute-start | bytes 12296 | tf_op jit(solution)/shard_map/ppermute | solution.py:28
  215.9 4.5 %collective-permute-done.21 = f32[4,2,128]{2,1,0:T(2,128)S(1)} collective-permute-done((f32[4,2,128]{2,1,0:T(2,128)S(1)}, f32[4,2,128]{2,1,0:T(2,128)S(1)}, u32[]{:S(2)}, u32[]{:S(2)}) %collective-permute-start.21) | collective-permute-done | bytes 4128 | tf_op jit(solution)/shard_map/ppermute | solution.py:30
  220.5 3.9 collective-permute-start.22
  231.5 11.8 %gather_fusion.3 = f32[2048]{0:T(1024)S(1)} fusion(f32[8192]{0:T(1024)S(1)} %add_bitcast_fusion.2, s32[2048]{0:T(1024)S(1)} %broadcast_clamp_fusion), kind=kCustom, calls=%fused_computation.3 | custom fusion | bytes 24576 | tf_op jit(solution)/shard_map/gather | solution.py:126
  243.3 3.6 scatter_fusion.3
  247.6 6.2 %all-to-all-start.5 = ((f32[16,1,256]{2,1,0:T(1,128)}), f32[16,1,256]{2,1,0:T(1,128)S(1)}, u32[]{:S(2)}, u32[]{:S(2)}) async-start(f32[16,1,256]{2,1,0:T(1,128)} %all_to_all.68), calls=%async_computation.5 | async-start | bytes 32768 | tf_op jit(solution)/shard_map/all_to_all | solution.py:128
  253.9 5.7 %all-to-all-done.5 = f32[16,1,256]{2,1,0:T(1,128)S(1)} async-done(((f32[16,1,256]{2,1,0:T(1,128)}), f32[16,1,256]{2,1,0:T(1,128)S(1)}, u32[]{:S(2)}, u32[]{:S(2)}) %all-to-all-start.5) | async-done | bytes 16416 | tf_op jit(solution)/shard_map/all_to_all | solution.py:128
  263.4 3.7 all-to-all-start.6
  267.2 5.8 %all-to-all-done.6 = f32[16,1,256]{2,1,0:T(1,128)S(1)} async-done(((f32[16,1,256]{2,1,0:T(1,128)}), f32[16,1,256]{2,1,0:T(1,128)S(1)}, u32[]{:S(2)}, u32[]{:S(2)}) %all-to-all-start.6) | async-done | bytes 16416 | tf_op jit(solution)/shard_map/all_to_all | solution.py:139
  273.9 14.5 %scatter_fusion.4 = f32[8192]{0:T(1024)S(1)} fusion(f32[8192]{0:T(1024)S(1)} %add_bitcast_fusion.2, s32[2048]{0:T(1024)S(1)} %reshape.590, f32[2048]{0:T(1024)S(1)} %reshape.614), kind=kCustom, calls=%fused_computation.17 | custom fusion | flops 2048 | bytes 32768 | tf_op jit(solution)/shard_map/scatter-add | solution.py:148
  291.0 3.7 collective-permute-start.25
  297.7 3.9 collective-permute-start.26
  308.6 11.8 %gather_fusion.6 = f32[2048]{0:T(1024)S(1)} fusion(f32[8192]{0:T(1024)S(1)} %add_bitcast_fusion.1, s32[2048]{0:T(1024)S(1)} %broadcast_clamp_fusion), kind=kCustom, calls=%fused_computation.6 | custom fusion | bytes 24576 | tf_op jit(solution)/shard_map/gather | solution.py:126
  320.5 3.6 scatter_fusion.5
  324.7 6.2 %all-to-all-start.8 = ((f32[16,1,256]{2,1,0:T(1,128)}), f32[16,1,256]{2,1,0:T(1,128)S(1)}, u32[]{:S(2)}, u32[]{:S(2)}) async-start(f32[16,1,256]{2,1,0:T(1,128)} %all_to_all.72), calls=%async_computation.8 | async-start | bytes 32768 | tf_op jit(solution)/shard_map/all_to_all | solution.py:128
  331.0 5.7 %all-to-all-done.8 = f32[16,1,256]{2,1,0:T(1,128)S(1)} async-done(((f32[16,1,256]{2,1,0:T(1,128)}), f32[16,1,256]{2,1,0:T(1,128)S(1)}, u32[]{:S(2)}, u32[]{:S(2)}) %all-to-all-start.8) | async-done | bytes 16416 | tf_op jit(solution)/shard_map/all_to_all | solution.py:128
  340.8 3.7 all-to-all-start.9
  344.6 5.8 %all-to-all-done.9 = f32[16,1,256]{2,1,0:T(1,128)S(1)} async-done(((f32[16,1,256]{2,1,0:T(1,128)}), f32[16,1,256]{2,1,0:T(1,128)S(1)}, u32[]{:S(2)}, u32[]{:S(2)}) %all-to-all-start.9) | async-done | bytes 16416 | tf_op jit(solution)/shard_map/all_to_all | solution.py:139
  351.3 14.5 %scatter_fusion.6 = f32[8192]{0:T(1024)S(1)} fusion(f32[8192]{0:T(1024)S(1)} %add_bitcast_fusion.1, s32[2048]{0:T(1024)S(1)} %reshape.590, f32[2048]{0:T(1024)S(1)} %reshape.636), kind=kCustom, calls=%fused_computation.20 | custom fusion | flops 2048 | bytes 32768 | tf_op jit(solution)/shard_map/scatter-add | solution.py:148
  375.8 3.9 collective-permute-start.30
  386.7 11.8 %gather_fusion.9 = f32[2048]{0:T(1024)S(1)} fusion(f32[8192]{0:T(1024)S(1)} %add_bitcast_fusion, s32[2048]{0:T(1024)S(1)} %broadcast_clamp_fusion), kind=kCustom, calls=%fused_computation.9 | custom fusion | bytes 24576 | tf_op jit(solution)/shard_map/gather | solution.py:126
  398.6 3.6 scatter_fusion.7
  402.9 6.2 %all-to-all-start.11 = ((f32[16,1,256]{2,1,0:T(1,128)}), f32[16,1,256]{2,1,0:T(1,128)S(1)}, u32[]{:S(2)}, u32[]{:S(2)}) async-start(f32[16,1,256]{2,1,0:T(1,128)} %all_to_all.76), calls=%async_computation.11 | async-start | bytes 32768 | tf_op jit(solution)/shard_map/all_to_all | solution.py:128
  409.2 5.7 %all-to-all-done.11 = f32[16,1,256]{2,1,0:T(1,128)S(1)} async-done(((f32[16,1,256]{2,1,0:T(1,128)}), f32[16,1,256]{2,1,0:T(1,128)S(1)}, u32[]{:S(2)}, u32[]{:S(2)}) %all-to-all-start.11) | async-done | bytes 16416 | tf_op jit(solution)/shard_map/all_to_all | solution.py:128
  416.9 3.7 all-to-all-start.12
  422.0 4.5 %all-to-all-done.12 = f32[16,1,256]{2,1,0:T(1,128)S(1)} async-done(((f32[16,1,256]{2,1,0:T(1,128)}), f32[16,1,256]{2,1,0:T(1,128)S(1)}, u32[]{:S(2)}, u32[]{:S(2)}) %all-to-all-start.12) | async-done | bytes 16416 | tf_op jit(solution)/shard_map/all_to_all | solution.py:139
  427.4 14.5 %scatter_fusion.8 = f32[8192]{0:T(1024)S(1)} fusion(f32[8192]{0:T(1024)S(1)} %add_bitcast_fusion, s32[2048]{0:T(1024)S(1)} %reshape.590, f32[2048]{0:T(1024)S(1)} %reshape.658), kind=kCustom, calls=%fused_computation.23 | custom fusion | flops 2048 | bytes 32768 | tf_op jit(solution)/shard_map/scatter-add | solution.py:148
  (325 shorter events, 129.4 us)
Async XLA Ops:
  0.6 28.9 %copy-start = (s32[1,16,2]{1,2,0:T(2,128)S(1)}, s32[1,16,2]{1,2,0:T(2,128)}, u32[]{:S(2)}) copy-start(s32[1,16,2]{1,2,0:T(2,128)} %param.29) | copy-start | bytes 388
  1.4 37.5 %collective-permute-start = (f32[4,2,128]{2,1,0:T(2,128)S(1)}, f32[4,2,128]{2,1,0:T(2,128)S(1)}, u32[]{:S(2)}, u32[]{:S(2)}) collective-permute-start(f32[4,2,128]{2,1,0:T(2,128)S(1)} %get-tuple-element.203), channel_id=1, source_target_pairs={{0,16},{16,32},{32,48},{48,64},{64,80},{80,96},{96,112},{112,128},... | collective-permute-start | bytes 12296 | tf_op jit(solution)/shard_map/ppermute | solution.py:28
  7.5 31.4 %collective-permute-start.1 = (f32[4,2,128]{2,1,0:T(2,128)S(1)}, f32[4,2,128]{2,1,0:T(2,128)S(1)}, u32[]{:S(2)}, u32[]{:S(2)}) collective-permute-start(f32[4,2,128]{2,1,0:T(2,128)S(1)} %get-tuple-element.204), channel_id=1, source_target_pairs={{16,0},{32,16},{48,32},{64,48},{80,64},{96,80},{112,96},{128,112},... | collective-permute-start | bytes 12296 | tf_op jit(solution)/shard_map/ppermute | solution.py:30
  10.4 34.6 %collective-permute-start.16 = (f32[4,2,128]{2,1,0:T(2,128)S(1)}, f32[4,2,128]{2,1,0:T(2,128)S(1)}, u32[]{:S(2)}, u32[]{:S(2)}) collective-permute-start(f32[4,2,128]{2,1,0:T(2,128)S(1)} %get-tuple-element.171), channel_id=1, source_target_pairs={{0,16},{16,32},{32,48},{48,64},{64,80},{80,96},{96,112},{112,128},... | collective-permute-start | bytes 12296 | tf_op jit(solution)/shard_map/ppermute | solution.py:28
  15.9 29.2 %collective-permute-start.17 = (f32[4,2,128]{2,1,0:T(2,128)S(1)}, f32[4,2,128]{2,1,0:T(2,128)S(1)}, u32[]{:S(2)}, u32[]{:S(2)}) collective-permute-start(f32[4,2,128]{2,1,0:T(2,128)S(1)} %get-tuple-element.172), channel_id=1, source_target_pairs={{16,0},{32,16},{48,32},{64,48},{80,64},{96,80},{112,96},{128,112},... | collective-permute-start | bytes 12296 | tf_op jit(solution)/shard_map/ppermute | solution.py:30
  18.9 11.2 %copy-start.12 = (s32[64]{0:T(128)S(1)}, s32[64]{0:T(128)}, u32[]{:S(2)}) copy-start(s32[64]{0:T(128)} %param.31) | copy-start | bytes 772
  18.9 11.2 %copy-start.13 = (s32[64]{0:T(128)S(1)}, s32[64]{0:T(128)}, u32[]{:S(2)}) copy-start(s32[64]{0:T(128)} %param.30) | copy-start | bytes 772
  23.1 14.5 %all-to-all-start.1 = ((f32[16,1,8]{2,1,0:T(1,128)}), f32[16,1,8]{2,1,0:T(1,128)S(1)}, u32[]{:S(2)}, u32[]{:S(2)}) async-start(f32[16,1,8]{2,1,0:T(1,128)} %copy.86), calls=%async_computation.1 | async-start | bytes 16384 | tf_op jit(solution)/shard_map/all_to_all | solution.py:135
  39.6 5.5 %collective-permute-start.2 = (f32[4,20,2]{2,1,0:T(8,128)S(1)}, f32[4,20,2]{2,1,0:T(8,128)S(1)}, u32[]{:S(2)}, u32[]{:S(2)}) collective-permute-start(f32[4,20,2]{2,1,0:T(8,128)S(1)} %get-tuple-element.195), channel_id=1, source_target_pairs={{0,1},{1,2},{2,3},{3,4},{4,5},{5,6},{6,7},{7,8},{8,9},{9,10},{10,1... | collective-permute-start | bytes 1928 | tf_op jit(solution)/shard_map/ppermute | solution.py:28
  43.2 5.4 %collective-permute-start.3 = (f32[4,20,2]{2,1,0:T(8,128)S(1)}, f32[4,20,2]{2,1,0:T(8,128)S(1)}, u32[]{:S(2)}, u32[]{:S(2)}) collective-permute-start(f32[4,20,2]{2,1,0:T(8,128)S(1)} %get-tuple-element.196), channel_id=1, source_target_pairs={{1,0},{2,1},{3,2},{4,3},{5,4},{6,5},{7,6},{8,7},{9,8},{10,9},{11,1... | collective-permute-start | bytes 1928 | tf_op jit(solution)/shard_map/ppermute | solution.py:30
  49.1 20.2 %collective-permute-start.4 = (f32[4,2,128]{2,1,0:T(2,128)S(1)}, f32[4,2,128]{2,1,0:T(2,128)S(1)}, u32[]{:S(2)}, u32[]{:S(2)}) collective-permute-start(f32[4,2,128]{2,1,0:T(2,128)S(1)} %get-tuple-element.201), channel_id=1, source_target_pairs={{0,16},{16,32},{32,48},{48,64},{64,80},{80,96},{96,112},{112,128},... | collective-permute-start | bytes 12296 | tf_op jit(solution)/shard_map/ppermute | solution.py:28
  54.8 14.5 %collective-permute-start.5 = (f32[4,2,128]{2,1,0:T(2,128)S(1)}, f32[4,2,128]{2,1,0:T(2,128)S(1)}, u32[]{:S(2)}, u32[]{:S(2)}) collective-permute-start(f32[4,2,128]{2,1,0:T(2,128)S(1)} %get-tuple-element.202), channel_id=1, source_target_pairs={{16,0},{32,16},{48,32},{64,48},{80,64},{96,80},{112,96},{128,112},... | collective-permute-start | bytes 12296 | tf_op jit(solution)/shard_map/ppermute | solution.py:30
  56.8 18.0 %collective-permute-start.18 = (f32[4,68,2]{2,1,0:T(8,128)S(1)}, f32[4,68,2]{2,1,0:T(8,128)S(1)}, u32[]{:S(2)}, u32[]{:S(2)}) collective-permute-start(f32[4,68,2]{2,1,0:T(8,128)S(1)} %get-tuple-element.143), channel_id=1, source_target_pairs={{0,1},{1,2},{2,3},{3,4},{4,5},{5,6},{6,7},{7,8},{8,9},{9,10},{10,1... | collective-permute-start | bytes 6536 | tf_op jit(solution)/shard_map/ppermute | solution.py:28
  59.0 15.8 %collective-permute-start.19 = (f32[4,68,2]{2,1,0:T(8,128)S(1)}, f32[4,68,2]{2,1,0:T(8,128)S(1)}, u32[]{:S(2)}, u32[]{:S(2)}) collective-permute-start(f32[4,68,2]{2,1,0:T(8,128)S(1)} %get-tuple-element.144), channel_id=1, source_target_pairs={{1,0},{2,1},{3,2},{4,3},{5,4},{6,5},{7,6},{8,7},{9,8},{10,9},{11,1... | collective-permute-start | bytes 6536 | tf_op jit(solution)/shard_map/ppermute | solution.py:30
  61.9 57.5 %all-to-all-start = ((f32[16,16,128]{2,1,0:T(8,128)}), f32[16,16,128]{2,1,0:T(8,128)S(1)}, u32[]{:S(2)}, u32[]{:S(2)}) async-start(f32[16,16,128]{2,1,0:T(8,128)} %stack.97), calls=%async_computation | async-start | bytes 262144 | tf_op jit(solution)/shard_map/all_to_all | solution.py:115
  69.4 5.7 %collective-permute-start.6 = (f32[4,20,2]{2,1,0:T(8,128)S(1)}, f32[4,20,2]{2,1,0:T(8,128)S(1)}, u32[]{:S(2)}, u32[]{:S(2)}) collective-permute-start(f32[4,20,2]{2,1,0:T(8,128)S(1)} %get-tuple-element.193), channel_id=1, source_target_pairs={{0,1},{1,2},{2,3},{3,4},{4,5},{5,6},{6,7},{7,8},{8,9},{9,10},{10,1... | collective-permute-start | bytes 1928 | tf_op jit(solution)/shard_map/ppermute | solution.py:28
  72.9 5.4 %collective-permute-start.7 = (f32[4,20,2]{2,1,0:T(8,128)S(1)}, f32[4,20,2]{2,1,0:T(8,128)S(1)}, u32[]{:S(2)}, u32[]{:S(2)}) collective-permute-start(f32[4,20,2]{2,1,0:T(8,128)S(1)} %get-tuple-element.194), channel_id=1, source_target_pairs={{1,0},{2,1},{3,2},{4,3},{5,4},{6,5},{7,6},{8,7},{9,8},{10,9},{11,1... | collective-permute-start | bytes 1928 | tf_op jit(solution)/shard_map/ppermute | solution.py:30
  78.8 7.7 %collective-permute-start.8 = (f32[4,2,128]{2,1,0:T(2,128)S(1)}, f32[4,2,128]{2,1,0:T(2,128)S(1)}, u32[]{:S(2)}, u32[]{:S(2)}) collective-permute-start(f32[4,2,128]{2,1,0:T(2,128)S(1)} %get-tuple-element.199), channel_id=1, source_target_pairs={{0,16},{16,32},{32,48},{48,64},{64,80},{80,96},{96,112},{112,128},... | collective-permute-start | bytes 12296 | tf_op jit(solution)/shard_map/ppermute | solution.py:28
  84.6 6.5 %collective-permute-start.9 = (f32[4,2,128]{2,1,0:T(2,128)S(1)}, f32[4,2,128]{2,1,0:T(2,128)S(1)}, u32[]{:S(2)}, u32[]{:S(2)}) collective-permute-start(f32[4,2,128]{2,1,0:T(2,128)S(1)} %get-tuple-element.200), channel_id=1, source_target_pairs={{16,0},{32,16},{48,32},{64,48},{80,64},{96,80},{112,96},{128,112},... | collective-permute-start | bytes 12296 | tf_op jit(solution)/shard_map/ppermute | solution.py:30
  91.1 5.4 %collective-permute-start.10 = (f32[4,20,2]{2,1,0:T(8,128)S(1)}, f32[4,20,2]{2,1,0:T(8,128)S(1)}, u32[]{:S(2)}, u32[]{:S(2)}) collective-permute-start(f32[4,20,2]{2,1,0:T(8,128)S(1)} %get-tuple-element.191), channel_id=1, source_target_pairs={{0,1},{1,2},{2,3},{3,4},{4,5},{5,6},{6,7},{7,8},{8,9},{9,10},{10,1... | collective-permute-start | bytes 1928 | tf_op jit(solution)/shard_map/ppermute | solution.py:28
  94.5 5.4 %collective-permute-start.11 = (f32[4,20,2]{2,1,0:T(8,128)S(1)}, f32[4,20,2]{2,1,0:T(8,128)S(1)}, u32[]{:S(2)}, u32[]{:S(2)}) collective-permute-start(f32[4,20,2]{2,1,0:T(8,128)S(1)} %get-tuple-element.192), channel_id=1, source_target_pairs={{1,0},{2,1},{3,2},{4,3},{5,4},{6,5},{7,6},{8,7},{9,8},{10,9},{11,1... | collective-permute-start | bytes 1928 | tf_op jit(solution)/shard_map/ppermute | solution.py:30
  100.4 6.3 %collective-permute-start.12 = (f32[4,2,128]{2,1,0:T(2,128)S(1)}, f32[4,2,128]{2,1,0:T(2,128)S(1)}, u32[]{:S(2)}, u32[]{:S(2)}) collective-permute-start(f32[4,2,128]{2,1,0:T(2,128)S(1)} %get-tuple-element.197), channel_id=1, source_target_pairs={{0,16},{16,32},{32,48},{48,64},{64,80},{80,96},{96,112},{112,128},... | collective-permute-start | bytes 12296 | tf_op jit(solution)/shard_map/ppermute | solution.py:28
  102.3 7.4 %collective-permute-start.13 = (f32[4,2,128]{2,1,0:T(2,128)S(1)}, f32[4,2,128]{2,1,0:T(2,128)S(1)}, u32[]{:S(2)}, u32[]{:S(2)}) collective-permute-start(f32[4,2,128]{2,1,0:T(2,128)S(1)} %get-tuple-element.198), channel_id=1, source_target_pairs={{16,0},{32,16},{48,32},{64,48},{80,64},{96,80},{112,96},{128,112},... | collective-permute-start | bytes 12296 | tf_op jit(solution)/shard_map/ppermute | solution.py:30
  109.8 5.1 %collective-permute-start.14 = (f32[4,20,2]{2,1,0:T(8,128)S(1)}, f32[4,20,2]{2,1,0:T(8,128)S(1)}, u32[]{:S(2)}, u32[]{:S(2)}) collective-permute-start(f32[4,20,2]{2,1,0:T(8,128)S(1)} %get-tuple-element.189), channel_id=1, source_target_pairs={{0,1},{1,2},{2,3},{3,4},{4,5},{5,6},{6,7},{7,8},{8,9},{9,10},{10,1... | collective-permute-start | bytes 1928 | tf_op jit(solution)/shard_map/ppermute | solution.py:28
  112.8 5.4 %collective-permute-start.15 = (f32[4,20,2]{2,1,0:T(8,128)S(1)}, f32[4,20,2]{2,1,0:T(8,128)S(1)}, u32[]{:S(2)}, u32[]{:S(2)}) collective-permute-start(f32[4,20,2]{2,1,0:T(8,128)S(1)} %get-tuple-element.190), channel_id=1, source_target_pairs={{1,0},{2,1},{3,2},{4,3},{5,4},{6,5},{7,6},{8,7},{9,8},{10,9},{11,1... | collective-permute-start | bytes 1928 | tf_op jit(solution)/shard_map/ppermute | solution.py:30
  120.0 27.1 %all-to-all-start.4 = ((f32[16,16,128]{2,1,0:T(8,128)}), f32[16,16,128]{2,1,0:T(8,128)S(1)}, u32[]{:S(2)}, u32[]{:S(2)}) async-start(f32[16,16,128]{2,1,0:T(8,128)} %stack.100), calls=%async_computation.4 | async-start | bytes 262144 | tf_op jit(solution)/shard_map/all_to_all | solution.py:115
  147.7 11.9 %all-to-all-start.7 = ((f32[16,16,128]{2,1,0:T(8,128)}), f32[16,16,128]{2,1,0:T(8,128)S(1)}, u32[]{:S(2)}, u32[]{:S(2)}) async-start(f32[16,16,128]{2,1,0:T(8,128)} %stack.213), calls=%async_computation.7 | async-start | bytes 262144 | tf_op jit(solution)/shard_map/all_to_all | solution.py:115
  160.3 10.2 %all-to-all-start.10 = ((f32[16,16,128]{2,1,0:T(8,128)}), f32[16,16,128]{2,1,0:T(8,128)S(1)}, u32[]{:S(2)}, u32[]{:S(2)}) async-start(f32[16,16,128]{2,1,0:T(8,128)} %stack.220), calls=%async_computation.10 | async-start | bytes 262144 | tf_op jit(solution)/shard_map/all_to_all | solution.py:115
  170.5 9.8 %all-to-all-start.2 = ((f32[16,1,256]{2,1,0:T(1,128)}), f32[16,1,256]{2,1,0:T(1,128)S(1)}, u32[]{:S(2)}, u32[]{:S(2)}) async-start(f32[16,1,256]{2,1,0:T(1,128)} %all_to_all.64), calls=%async_computation.2 | async-start | bytes 32768 | tf_op jit(solution)/shard_map/all_to_all | solution.py:128
  184.1 9.5 %all-to-all-start.3 = ((f32[16,1,256]{2,1,0:T(1,128)}), f32[16,1,256]{2,1,0:T(1,128)S(1)}, u32[]{:S(2)}, u32[]{:S(2)}) async-start(f32[16,1,256]{2,1,0:T(1,128)} %mul.476), calls=%async_computation.3 | async-start | bytes 32768 | tf_op jit(solution)/shard_map/all_to_all | solution.py:139
  209.4 6.6 %collective-permute-start.20 = (f32[4,2,128]{2,1,0:T(2,128)S(1)}, f32[4,2,128]{2,1,0:T(2,128)S(1)}, u32[]{:S(2)}, u32[]{:S(2)}) collective-permute-start(f32[4,2,128]{2,1,0:T(2,128)S(1)} %get-tuple-element.167), channel_id=1, source_target_pairs={{0,16},{16,32},{32,48},{48,64},{64,80},{80,96},{96,112},{112,128},... | collective-permute-start | bytes 12296 | tf_op jit(solution)/shard_map/ppermute | solution.py:28
  213.9 6.5 %collective-permute-start.21 = (f32[4,2,128]{2,1,0:T(2,128)S(1)}, f32[4,2,128]{2,1,0:T(2,128)S(1)}, u32[]{:S(2)}, u32[]{:S(2)}) collective-permute-start(f32[4,2,128]{2,1,0:T(2,128)S(1)} %get-tuple-element.168), channel_id=1, source_target_pairs={{16,0},{32,16},{48,32},{64,48},{80,64},{96,80},{112,96},{128,112},... | collective-permute-start | bytes 12296 | tf_op jit(solution)/shard_map/ppermute | solution.py:30
  220.5 7.2 %collective-permute-start.22 = (f32[4,68,2]{2,1,0:T(8,128)S(1)}, f32[4,68,2]{2,1,0:T(8,128)S(1)}, u32[]{:S(2)}, u32[]{:S(2)}) collective-permute-start(f32[4,68,2]{2,1,0:T(8,128)S(1)} %get-tuple-element.141), channel_id=1, source_target_pairs={{0,1},{1,2},{2,3},{3,4},{4,5},{5,6},{6,7},{7,8},{8,9},{9,10},{10,1... | collective-permute-start | bytes 6536 | tf_op jit(solution)/shard_map/ppermute | solution.py:28
  224.4 6.5 %collective-permute-start.23 = (f32[4,68,2]{2,1,0:T(8,128)S(1)}, f32[4,68,2]{2,1,0:T(8,128)S(1)}, u32[]{:S(2)}, u32[]{:S(2)}) collective-permute-start(f32[4,68,2]{2,1,0:T(8,128)S(1)} %get-tuple-element.142), channel_id=1, source_target_pairs={{1,0},{2,1},{3,2},{4,3},{5,4},{6,5},{7,6},{8,7},{9,8},{10,9},{11,1... | collective-permute-start | bytes 6536 | tf_op jit(solution)/shard_map/ppermute | solution.py:30
  247.6 12.0 %all-to-all-start.5 = ((f32[16,1,256]{2,1,0:T(1,128)}), f32[16,1,256]{2,1,0:T(1,128)S(1)}, u32[]{:S(2)}, u32[]{:S(2)}) async-start(f32[16,1,256]{2,1,0:T(1,128)} %all_to_all.68), calls=%async_computation.5 | async-start | bytes 32768 | tf_op jit(solution)/shard_map/all_to_all | solution.py:128
  263.4 9.5 %all-to-all-start.6 = ((f32[16,1,256]{2,1,0:T(1,128)}), f32[16,1,256]{2,1,0:T(1,128)S(1)}, u32[]{:S(2)}, u32[]{:S(2)}) async-start(f32[16,1,256]{2,1,0:T(1,128)} %mul.477), calls=%async_computation.6 | async-start | bytes 32768 | tf_op jit(solution)/shard_map/all_to_all | solution.py:139
  288.5 6.3 %collective-permute-start.24 = (f32[4,2,128]{2,1,0:T(2,128)S(1)}, f32[4,2,128]{2,1,0:T(2,128)S(1)}, u32[]{:S(2)}, u32[]{:S(2)}) collective-permute-start(f32[4,2,128]{2,1,0:T(2,128)S(1)} %get-tuple-element.161), channel_id=1, source_target_pairs={{0,16},{16,32},{32,48},{48,64},{64,80},{80,96},{96,112},{112,128},... | collective-permute-start | bytes 12296 | tf_op jit(solution)/shard_map/ppermute | solution.py:28
  291.0 6.5 %collective-permute-start.25 = (f32[4,2,128]{2,1,0:T(2,128)S(1)}, f32[4,2,128]{2,1,0:T(2,128)S(1)}, u32[]{:S(2)}, u32[]{:S(2)}) collective-permute-start(f32[4,2,128]{2,1,0:T(2,128)S(1)} %get-tuple-element.162), channel_id=1, source_target_pairs={{16,0},{32,16},{48,32},{64,48},{80,64},{96,80},{112,96},{128,112},... | collective-permute-start | bytes 12296 | tf_op jit(solution)/shard_map/ppermute | solution.py:30
  297.7 7.2 %collective-permute-start.26 = (f32[4,68,2]{2,1,0:T(8,128)S(1)}, f32[4,68,2]{2,1,0:T(8,128)S(1)}, u32[]{:S(2)}, u32[]{:S(2)}) collective-permute-start(f32[4,68,2]{2,1,0:T(8,128)S(1)} %get-tuple-element.139), channel_id=1, source_target_pairs={{0,1},{1,2},{2,3},{3,4},{4,5},{5,6},{6,7},{7,8},{8,9},{9,10},{10,1... | collective-permute-start | bytes 6536 | tf_op jit(solution)/shard_map/ppermute | solution.py:28
  301.5 6.5 %collective-permute-start.27 = (f32[4,68,2]{2,1,0:T(8,128)S(1)}, f32[4,68,2]{2,1,0:T(8,128)S(1)}, u32[]{:S(2)}, u32[]{:S(2)}) collective-permute-start(f32[4,68,2]{2,1,0:T(8,128)S(1)} %get-tuple-element.140), channel_id=1, source_target_pairs={{1,0},{2,1},{3,2},{4,3},{5,4},{6,5},{7,6},{8,7},{9,8},{10,9},{11,1... | collective-permute-start | bytes 6536 | tf_op jit(solution)/shard_map/ppermute | solution.py:30
  324.7 12.0 %all-to-all-start.8 = ((f32[16,1,256]{2,1,0:T(1,128)}), f32[16,1,256]{2,1,0:T(1,128)S(1)}, u32[]{:S(2)}, u32[]{:S(2)}) async-start(f32[16,1,256]{2,1,0:T(1,128)} %all_to_all.72), calls=%async_computation.8 | async-start | bytes 32768 | tf_op jit(solution)/shard_map/all_to_all | solution.py:128
  340.8 9.5 %all-to-all-start.9 = ((f32[16,1,256]{2,1,0:T(1,128)}), f32[16,1,256]{2,1,0:T(1,128)S(1)}, u32[]{:S(2)}, u32[]{:S(2)}) async-start(f32[16,1,256]{2,1,0:T(1,128)} %mul.478), calls=%async_computation.9 | async-start | bytes 32768 | tf_op jit(solution)/shard_map/all_to_all | solution.py:139
  365.9 6.3 %collective-permute-start.28 = (f32[4,2,128]{2,1,0:T(2,128)S(1)}, f32[4,2,128]{2,1,0:T(2,128)S(1)}, u32[]{:S(2)}, u32[]{:S(2)}) collective-permute-start(f32[4,2,128]{2,1,0:T(2,128)S(1)} %get-tuple-element.155), channel_id=1, source_target_pairs={{0,16},{16,32},{32,48},{48,64},{64,80},{80,96},{96,112},{112,128},... | collective-permute-start | bytes 12296 | tf_op jit(solution)/shard_map/ppermute | solution.py:28
  369.2 6.5 %collective-permute-start.29 = (f32[4,2,128]{2,1,0:T(2,128)S(1)}, f32[4,2,128]{2,1,0:T(2,128)S(1)}, u32[]{:S(2)}, u32[]{:S(2)}) collective-permute-start(f32[4,2,128]{2,1,0:T(2,128)S(1)} %get-tuple-element.156), channel_id=1, source_target_pairs={{16,0},{32,16},{48,32},{64,48},{80,64},{96,80},{112,96},{128,112},... | collective-permute-start | bytes 12296 | tf_op jit(solution)/shard_map/ppermute | solution.py:30
  375.8 7.2 %collective-permute-start.30 = (f32[4,68,2]{2,1,0:T(8,128)S(1)}, f32[4,68,2]{2,1,0:T(8,128)S(1)}, u32[]{:S(2)}, u32[]{:S(2)}) collective-permute-start(f32[4,68,2]{2,1,0:T(8,128)S(1)} %get-tuple-element.137), channel_id=1, source_target_pairs={{0,1},{1,2},{2,3},{3,4},{4,5},{5,6},{6,7},{7,8},{8,9},{9,10},{10,1... | collective-permute-start | bytes 6536 | tf_op jit(solution)/shard_map/ppermute | solution.py:28
  379.7 6.5 %collective-permute-start.31 = (f32[4,68,2]{2,1,0:T(8,128)S(1)}, f32[4,68,2]{2,1,0:T(8,128)S(1)}, u32[]{:S(2)}, u32[]{:S(2)}) collective-permute-start(f32[4,68,2]{2,1,0:T(8,128)S(1)} %get-tuple-element.138), channel_id=1, source_target_pairs={{1,0},{2,1},{3,2},{4,3},{5,4},{6,5},{7,6},{8,7},{9,8},{10,9},{11,1... | collective-permute-start | bytes 6536 | tf_op jit(solution)/shard_map/ppermute | solution.py:30
  402.9 12.0 %all-to-all-start.11 = ((f32[16,1,256]{2,1,0:T(1,128)}), f32[16,1,256]{2,1,0:T(1,128)S(1)}, u32[]{:S(2)}, u32[]{:S(2)}) async-start(f32[16,1,256]{2,1,0:T(1,128)} %all_to_all.76), calls=%async_computation.11 | async-start | bytes 32768 | tf_op jit(solution)/shard_map/all_to_all | solution.py:128
  416.9 9.5 %all-to-all-start.12 = ((f32[16,1,256]{2,1,0:T(1,128)}), f32[16,1,256]{2,1,0:T(1,128)S(1)}, u32[]{:S(2)}, u32[]{:S(2)}) async-start(f32[16,1,256]{2,1,0:T(1,128)} %mul.479), calls=%async_computation.12 | async-start | bytes 32768 | tf_op jit(solution)/shard_map/all_to_all | solution.py:139
  (12 other events, 42.0 us)
